TPU v7x, 32 devices: a whole 2x2x4 slice. The times are simulated.
32 devices in a mesh: row: 4 (over z), col: 8 (over y, x, core).
Axes of the slice: x: 2, y: 2, z: 4, core: 2. Of those that a mesh axis runs over, the one named last changes fastest.
Arguments:
- tokens: bfloat16 [2560, 8192], P('row', 'col'), may hold values from -6 to 6
- norm_gain: bfloat16 [8192], replicated, may hold values from 0.099609375 to 1.8984375
- w_query: bfloat16 [8192, 8192], P('row', 'col')
- w_key: bfloat16 [8192, 1024], P('row')
- w_value: bfloat16 [8192, 1024], P('row'), may hold values from -0.0625 to 0.0625
- w_out: bfloat16 [8192, 8192], P('row', 'col'), may hold values from -0.0625 to 0.0625
- doc_lengths: int32 [4], replicated, may hold values from 1 to 1280, 2560 in all
Outputs:
- layer_out: bfloat16 [2560, 8192], P('row', 'col')
Inputs may be any that keep to these rules, and one draw needn't show every extreme that they name: `doc_lengths`: positive lengths that add up to 2560; the largest is exactly 1280.
All inputs are finite; a program needn't handle non-finite values.
Results may differ from a plain program's by a relative error of at most 0.011.
Values may be sent and summed in bfloat16 or wider, within the bound.
No kernel may reach another device: no remote copies, remote signals or barrier semaphores. Data moves between devices by JAX's collectives and lax.ppermute only.
A program may use at most 192 MiB of HBM per device.

v0:
```python
import jax
import jax.numpy as jnp
from jax import lax
from jax.sharding import PartitionSpec as P

HEADS = 64
KVH = 8
HD = 128
rope_base = 500000.0
norm_eps = 1e-05
masked_value = -1e30


def rope_tables(positions, head_dim):
    freq_index = jnp.arange(head_dim // 2, dtype=jnp.int32).astype(jnp.float32)
    inverse = rope_base ** (-2.0 * freq_index / head_dim)
    angles = positions.astype(jnp.float32)[:, None] * inverse[None, :]
    return (jnp.cos(angles), jnp.sin(angles))


def rotate(vectors, cosine, sine):
    half_dim = vectors.shape[-1] // 2
    first = vectors[..., :half_dim]
    second = vectors[..., half_dim:]
    cos_part = cosine[:, None, :]
    sin_part = sine[:, None, :]
    return jnp.concatenate(
        [first * cos_part - second * sin_part, second * cos_part + first * sin_part], axis=-1
    )


def doc_index(positions, doc_ends):
    return jnp.sum((positions[:, None] >= doc_ends[None, :]).astype(jnp.int32), axis=1)


def body(tokens, norm_gain, w_query, w_key, w_value, w_out, doc_lengths):
    tok_rows = tokens.shape[0]
    col_index = lax.axis_index("col")
    row_index = lax.axis_index("row")
    query_cols = w_query.shape[1]
    local_heads = query_cols // HD
    group_size = HEADS // KVH
    kv_head = col_index * local_heads // group_size
    key_cols = lax.dynamic_slice_in_dim(w_key, kv_head * HD, HD, 1)
    value_cols = lax.dynamic_slice_in_dim(w_value, kv_head * HD, HD, 1)
    gathered = lax.all_gather(tokens, "col", axis=1, tiled=True)
    whole_f = gathered.astype(jnp.float32)
    whole_rms = lax.rsqrt(jnp.mean(whole_f * whole_f, axis=1, keepdims=True) + norm_eps)
    normed = (whole_f * whole_rms * norm_gain.astype(jnp.float32)[None, :]).astype(jnp.bfloat16)
    queries = jnp.dot(
        normed,
        lax.all_gather(w_query, "row", axis=0, tiled=True),
        preferred_element_type=jnp.float32,
    )
    keys_f = jnp.dot(
        normed,
        lax.all_gather(key_cols, "row", axis=0, tiled=True),
        preferred_element_type=jnp.float32,
    )
    values_f = jnp.dot(
        normed,
        lax.all_gather(value_cols, "row", axis=0, tiled=True),
        preferred_element_type=jnp.float32,
    )
    positions = row_index * tok_rows + jnp.arange(tok_rows, dtype=jnp.int32)
    cosine, sine = rope_tables(positions, HD)
    q_rot = rotate(queries.reshape(tok_rows, local_heads, HD), cosine, sine).astype(jnp.bfloat16)
    k_rot = (
        rotate(keys_f.reshape(tok_rows, 1, HD), cosine, sine)
        .reshape(tok_rows, HD)
        .astype(jnp.bfloat16)
    )
    v_cast = values_f.astype(jnp.bfloat16)
    doc_ends = jnp.cumsum(doc_lengths)
    query_docs = doc_index(positions, doc_ends)
    score_scale = HD ** (-0.5)
    start_state = (
        jnp.full((local_heads, tok_rows), masked_value, jnp.float32),
        jnp.zeros((local_heads, tok_rows), jnp.float32),
        jnp.zeros((local_heads, tok_rows, HD), jnp.float32),
    )
    key_piece = lax.all_gather(k_rot, "row", axis=0, tiled=True)
    value_piece = lax.all_gather(v_cast, "row", axis=0, tiled=True)
    blocks = key_piece.shape[0] // tok_rows
    key_blocks = key_piece.reshape(blocks, tok_rows, HD)
    value_blocks = value_piece.reshape(blocks, tok_rows, HD)

    def visit(state, block_in):
        key_block, value_block, block_number = block_in
        run_max, run_total, run_acc = state
        key_pos = block_number * tok_rows + jnp.arange(tok_rows, dtype=jnp.int32)
        allowed = (query_docs[:, None] == doc_index(key_pos, doc_ends)[None, :]) & (
            key_pos[None, :] <= positions[:, None]
        )
        scores = (
            jnp.einsum("qhd,kd->hqk", q_rot, key_block, preferred_element_type=jnp.float32)
            * score_scale
        )
        masked = jnp.where(allowed[None], scores, masked_value)
        new_max = jnp.maximum(run_max, jnp.max(masked, axis=2))
        factor = jnp.exp(run_max - new_max)
        weights = jnp.where(allowed[None], jnp.exp(masked - new_max[:, :, None]), 0.0)
        new_total = run_total * factor + jnp.sum(weights, axis=2)
        new_acc = run_acc * factor[:, :, None] + jnp.einsum(
            "hqk,kd->hqd",
            weights.astype(jnp.bfloat16),
            value_block,
            preferred_element_type=jnp.float32,
        )
        return ((new_max, new_total, new_acc), None)

    final_state, unused = lax.scan(
        visit, start_state, (key_blocks, value_blocks, jnp.arange(blocks, dtype=jnp.int32))
    )
    run_max, run_total, run_acc = final_state
    context = (
        (run_acc / run_total[:, :, None])
        .astype(jnp.bfloat16)
        .transpose(1, 0, 2)
        .reshape(tok_rows, query_cols)
    )
    weight_whole = lax.all_gather(w_out, "row", axis=0, tiled=True)
    projected = jnp.dot(
        lax.all_gather(context, "col", axis=1, tiled=True),
        weight_whole,
        preferred_element_type=jnp.float32,
    )
    return (tokens.astype(jnp.float32) + projected).astype(jnp.bfloat16)


def solution(mesh):
    return jax.shard_map(
        body,
        mesh=mesh,
        in_specs=(
            P("row", "col"),
            P(),
            P("row", "col"),
            P("row", None),
            P("row", None),
            P("row", "col"),
            P(),
        ),
        out_specs=P("row", "col"),
        check_vma=False,
    )
```

profile of v0, /device:TPU:0, one launch (start us, length us, event | category | flops | bytes accessed | tf_op | source)
XLA Modules:
  0.0 848.5 jit_solution(15458748518854976077)
XLA Ops:
  7.3 1.9 constant_dynamic-slice_fusion.1
  9.3 1.9 constant_dynamic-slice_fusion
  12.7 1.2 multiply_cosine_fusion
  14.0 61.2 %all-gather.8.cloned.1.call-done = bf16[640,8192]{1,0:T(8,128)(2,1)} async-done(((bf16[640,1024]{1,0:T(8,128)(2,1)}), bf16[640,8192]{1,0:T(8,128)(2,1)}) %all-gather.8.cloned.1.call-update) | async-done | bytes 10485776 | tf_op jit(solution)/shard_map/all_gather | solution.py:46
  75.3 6.1 fusion.22
  81.4 41.4 %all-gather.10.cloned.1.call-done = bf16[8192,128]{1,0:T(8,128)(2,1)} async-done(((bf16[2048,128]{1,0:T(8,128)(2,1)}), bf16[8192,128]{1,0:T(8,128)(2,1)}) %all-gather.10.cloned.1.call-update) | async-done | bytes 2097168 | tf_op jit(solution)/shard_map/all_gather | solution.py:57
  122.8 7.8 convolution_bitcast_fusion.1
  131.3 26.0 %all-gather = bf16[2560,1,128]{0,2,1:T(8,128)(2,1)S(1)} all-gather(bf16[640,1,128]{0,2,1:T(8,128)(2,1)S(1)} %pad_maximum_fusion.1), channel_id=2, replica_groups=mesh['row'=4,'col'=8] {'row'}, dimensions={0}, use_global_device_ids=true | all-gather | bytes 819200 | tf_op jit(solution)/shard_map/all_gather | solution.py:82
  157.7 21.4 %all-gather.14.cloned.1.call-done = bf16[8192,128]{1,0:T(8,128)(2,1)} async-done(((bf16[2048,128]{1,0:T(8,128)(2,1)}), bf16[8192,128]{1,0:T(8,128)(2,1)}) %all-gather.14.cloned.1.call-update) | async-done | bytes 2097168 | tf_op jit(solution)/shard_map/all_gather | solution.py:62
  179.1 7.5 convolution_convert_fusion
  186.6 38.9 %all_gather.29 = bf16[2560,128]{1,0:T(8,128)(2,1)} all-gather(bf16[640,128]{1,0:T(8,128)(2,1)S(1)} %convolution_convert_fusion), channel_id=1, replica_groups=mesh['row'=4,'col'=8] {'row'}, dimensions={0}, use_global_device_ids=true | all-gather | bytes 819200 | tf_op jit(solution)/shard_map/all_gather | solution.py:83
  225.4 246.9 %all-gather.12.cloned.1.call-done = bf16[8192,1024]{1,0:T(8,128)(2,1)} async-done(((bf16[2048,1024]{1,0:T(8,128)(2,1)}), bf16[8192,1024]{1,0:T(8,128)(2,1)}) %all-gather.12.cloned.1.call-update) | async-done | bytes 16777232 | tf_op jit(solution)/shard_map/all_gather | solution.py:52
  472.4 16.2 %convolution_bitcast_fusion = f32[80,8,8,128]{3,1,2,0:T(8,128)S(1)} fusion(bf16[8192,1024]{1,0:T(8,128)(2,1)} %all-gather.12.cloned.1.call-done, bf16[640,8192]{1,0:T(8,128)(2,1)} %all-gather.8.cloned.1.call-done, f32[8192]{0:T(1024)S(1)} %convert_element_type.54, f32[640]{0:T(1024)S(1)} %add_rsqrt_fusion), kind=kOutput, calls=%fused_computation.37 | convolution fusion | flops 10758389760 | bytes 29919744 | tf_op jit(solution)/shard_map/dot_general | solution.py:50
  491.1 1.8 pad_maximum_fusion
  492.9 95.6 %while.15 = (s32[]{:T(128)}, f32[8,640]{1,0:T(8,128)S(1)}, f32[8,640]{1,0:T(8,128)S(1)}, f32[8,640,128]{2,1,0:T(8,128)}, s32[640]{0:T(1024)S(1)}, /*index=5*/s32...) while((s32[]{:T(128)}, f32[8,640]{1,0:T(8,128)S(1)}, ...), condition=%wide.region_7.8_spmd.clone, body=%wide.region_3.7_spmd.clone.sunk | while | flops 1723548800 | bytes 100618976 | solution.py:112
  494.6 7.3 fusion.54
  501.9 8.1 fusion.55
  510.5 6.0 fusion.57
  518.2 7.3 fusion.54
  525.6 8.0 fusion.55
  534.1 6.4 fusion.57
  542.2 7.3 fusion.54
  549.6 8.0 fusion.55
  558.0 6.4 fusion.57
  566.2 7.3 fusion.54
  573.5 8.0 fusion.55
  582.0 6.4 fusion.57
  588.5 2.1 copy.21
  590.6 1.3 divide_convert_fusion
  591.9 167.7 %all-gather.18.cloned.1.call-done = bf16[8192,1024]{1,0:T(8,128)(2,1)} async-done(((bf16[2048,1024]{1,0:T(8,128)(2,1)}), bf16[8192,1024]{1,0:T(8,128)(2,1)}) %all-gather.18.cloned.1.call-update) | async-done | bytes 16777232 | tf_op jit(solution)/shard_map/all_gather | solution.py:122
  759.6 63.2 %all-gather.16.cloned.1.call-done = bf16[640,8192]{0,1:T(8,128)(2,1)} async-done(((bf16[640,1024]{0,1:T(8,128)(2,1)}), bf16[640,8192]{0,1:T(8,128)(2,1)}) %all-gather.16.cloned.1.call-update) | async-done | bytes 10485776 | tf_op jit(solution)/shard_map/all_gather | solution.py:124
  822.9 18.8 %add_convert_fusion = bf16[640,1024]{1,0:T(8,128)(2,1)} fusion(bf16[640,1024]{1,0:T(8,128)(2,1)} %param.9, bf16[640,8192]{0,1:T(8,128)(2,1)} %all-gather.16.cloned.1.call-done, bf16[8192,1024]{1,0:T(8,128)(2,1)} %all-gather.18.cloned.1.call-done), kind=kOutput, calls=%fused_computation.33 | convolution fusion | flops 10739384320 | bytes 29884416 | tf_op jit(solution)/shard_map/dot_general | solution.py:123
  (69 shorter events, 12.1 us)
Async XLA Ops:
  6.5 68.7 %all-gather.8.cloned.1.call-start = ((), (), s32[]{:S(2)}) async-start(), calls=%async_computation | async-start | bytes 11796480 | tf_op jit(solution)/shard_map/all_gather | solution.py:46
  7.3 115.5 %all-gather.10.cloned.1.call-start = ((), (), s32[]{:S(2)}) async-start(), calls=%async_computation.1 | async-start | bytes 2621440 | tf_op jit(solution)/shard_map/all_gather | solution.py:57
  9.2 169.8 %all-gather.14.cloned.1.call-start = ((), (), s32[]{:S(2)}) async-start(), calls=%async_computation.3 | async-start | bytes 2621440 | tf_op jit(solution)/shard_map/all_gather | solution.py:62
  11.2 1.3 copy-start.2
  11.2 2.8 copy-start.1
  11.2 461.1 %all-gather.12.cloned.1.call-start = ((), (), s32[]{:S(2)}) async-start(), calls=%async_computation.2 | async-start | bytes 20971520 | tf_op jit(solution)/shard_map/all_gather | solution.py:52
  11.8 747.8 %all-gather.18.cloned.1.call-start = ((), (), s32[]{:S(2)}) async-start(), calls=%async_computation.5 | async-start | bytes 20971520 | tf_op jit(solution)/shard_map/all_gather | solution.py:122
  12.4 810.5 %all-gather.16.cloned.1.call-start = ((), (), s32[]{:S(2)}) async-start(), calls=%async_computation.4 | async-start | bytes 11796480 | tf_op jit(solution)/shard_map/all_gather | solution.py:124
  501.9 8.5 %copy-start = (f32[640,640,8]{1,0,2:T(8,128)S(1)}, f32[640,640,8]{1,0,2:T(8,128)}, u32[]{:S(2)}) copy-start(f32[640,640,8]{1,0,2:T(8,128)} %get-tuple-element.249) | copy-start | bytes 39321604 | tf_op jit(solution)/shard_map/while
  525.6 8.5 %copy-start = (f32[640,640,8]{1,0,2:T(8,128)S(1)}, f32[640,640,8]{1,0,2:T(8,128)}, u32[]{:S(2)}) copy-start(f32[640,640,8]{1,0,2:T(8,128)} %get-tuple-element.249) | copy-start | bytes 39321604 | tf_op jit(solution)/shard_map/while
  549.6 8.5 copy-start
  573.5 8.5 %copy-start = (f32[640,640,8]{1,0,2:T(8,128)S(1)}, f32[640,640,8]{1,0,2:T(8,128)}, u32[]{:S(2)}) copy-start(f32[640,640,8]{1,0,2:T(8,128)} %get-tuple-element.249) | copy-start | bytes 39321604 | tf_op jit(solution)/shard_map/while
Sparse Core Ops, SparseCore 0:
  9.3 65.9 all-gather.7
  76.8 45.9 all-gather.9
  124.4 54.6 all-gather.13
  180.5 291.8 all-gather.11
  473.8 285.8 all-gather.17
  761.4 61.4 all-gather.15
where the time goes:
time: 849 us; the launch traced here: 848 us
  waiting for transfers between devices  604 us (71%)
  matrix products  105 us (12%)
  blocking collectives  64.9 us (8%)
  other arithmetic  46.4 us (5%)
  between operations  13.7 us (2%)
  local copies, waits for them, and re-layouts  12 us (1%)
    all_gather x1, waiting for transfers between devices, body(): lax.all_gather(w_query, 'row', axis=0, tiled=True)  247 us
    all_gather x1, waiting for transfers between devices, body(): weight_whole = lax.all_gather(w_out, 'row', axis=0, tiled=True)  168 us
    all_gather x1, waiting for transfers between devices, body(): lax.all_gather(context, 'col', axis=1, tiled=True)  63.2 us
    all_gather x1, waiting for transfers between devices, body(): gathered = lax.all_gather(tokens, 'col', axis=1, tiled=True)  61.2 us
    all_gather x1, waiting for transfers between devices, body(): lax.all_gather(key_cols, 'row', axis=0, tiled=True)  41.4 us
    all_gather x1, blocking collectives, body(): value_piece = lax.all_gather(v_cast, 'row', axis=0, tiled=True)  38.9 us
    reduce_sum x4, other arithmetic, visit(): new_total = run_total * factor + jnp.sum(weights, axis=2)  32 us
    dot_general x4, matrix products, visit(): jnp.einsum('qhd,kd->hqk', q_rot, key_block, preferred_element_type=jnp.fl...  29.3 us
  transfers between devices with their start and end apart: 6, of which 6 were waited for; matrix products, arithmetic and copies ran while one was open for 17% of the time, Pallas kernels for 0%

commit v1 on v0

--- a/solution.py
+++ b/solution.py
@@ -79,8 +79,16 @@
         jnp.zeros((local_heads, tok_rows), jnp.float32),
         jnp.zeros((local_heads, tok_rows, HD), jnp.float32),
     )
-    key_piece = lax.all_gather(k_rot, "row", axis=0, tiled=True)
-    value_piece = lax.all_gather(v_cast, "row", axis=0, tiled=True)
+
+    def _attach_spot(frame, field_in):
+        d_next = jnp.split(
+            lax.all_gather(jnp.concatenate([field_in, frame], 1), "row", axis=0, tiled=True),
+            [field_in.shape[1]],
+            1,
+        )
+        return d_next
+
+    key_piece, value_piece = _attach_spot(v_cast, k_rot)
     blocks = key_piece.shape[0] // tok_rows
     key_blocks = key_piece.reshape(blocks, tok_rows, HD)
     value_blocks = value_piece.reshape(blocks, tok_rows, HD)

time: 849 us -> 872 us (1.027)
  waiting for transfers between devices: 604 us -> 689 us
  blocking collectives: 64.9 us -> 0 us
    all_gather x2 -> x0, blocking collectives: 64.9 us -> none  [the longest x1 38.9 us: body(): value_piece = lax.all_gather(v_cast, 'row', axis=0, tiled=True)]
    all_gather x1, waiting for transfers between devices: 247 us -> 285 us  [body(): lax.all_gather(w_query, 'row', axis=0, tiled=True)]
    all_gather x0 -> x1, waiting for transfers between devices: none -> 28.3 us  [_attach_spot(): lax.all_gather(jnp.concatenate([field_in, frame], 1), 'row', axis=0, tile...]
    all_gather x1, waiting for transfers between devices: 21.4 us -> 37.6 us  [body(): lax.all_gather(value_cols, 'row', axis=0, tiled=True)]
  transfers between devices with their start and end apart: 6 -> 7, of which waited for: 6 -> 7; matrix products, arithmetic and copies ran while one was open for 17% -> 16% of each run, Pallas kernels for 0% -> 0%
where the time goes in v1:
time: 872 us
  waiting for transfers between devices  689 us (79%)
  matrix products  105 us (12%)
  other arithmetic  47.1 us (5%)
  local copies, waits for them, and re-layouts  14.4 us (2%)
  between operations  13.7 us (2%)
    all_gather x1, waiting for transfers between devices, body(): lax.all_gather(w_query, 'row', axis=0, tiled=True)  285 us
    all_gather x1, waiting for transfers between devices, body(): weight_whole = lax.all_gather(w_out, 'row', axis=0, tiled=True)  167 us
    all_gather x1, waiting for transfers between devices, body(): gathered = lax.all_gather(tokens, 'col', axis=1, tiled=True)  64 us
    all_gather x1, waiting for transfers between devices, body(): lax.all_gather(context, 'col', axis=1, tiled=True)  63.4 us
    all_gather x1, waiting for transfers between devices, body(): lax.all_gather(key_cols, 'row', axis=0, tiled=True)  41.4 us
    all_gather x1, waiting for transfers between devices, body(): lax.all_gather(value_cols, 'row', axis=0, tiled=True)  37.6 us
    reduce_sum x4, other arithmetic, visit(): new_total = run_total * factor + jnp.sum(weights, axis=2)  32 us
    dot_general x4, matrix products, visit(): jnp.einsum('qhd,kd->hqk', q_rot, key_block, preferred_element_type=jnp.fl...  29.3 us
  transfers between devices with their start and end apart: 7, of which 7 were waited for; matrix products, arithmetic and copies ran while one was open for 16% of the time, Pallas kernels for 0%

profile of v1, /device:TPU:0, one launch (start us, length us, event | category | flops | bytes accessed | tf_op | source)
XLA Modules:
  0.0 871.9 jit_solution(13127976906965144968)
XLA Ops:
  7.3 1.9 constant_dynamic-slice_fusion.1
  9.3 1.9 constant_dynamic-slice_fusion
  11.3 64.0 %all-gather.8.cloned.1.call-done = bf16[640,8192]{1,0:T(8,128)(2,1)} async-done(((bf16[640,1024]{1,0:T(8,128)(2,1)}), bf16[640,8192]{1,0:T(8,128)(2,1)}) %all-gather.8.cloned.1.call-update) | async-done | bytes 10485776 | tf_op jit(solution)/shard_map/all_gather | solution.py:46
  75.3 6.1 fusion.22
  81.4 41.4 %all-gather.10.cloned.1.call-done = bf16[8192,128]{1,0:T(8,128)(2,1)} async-done(((bf16[2048,128]{1,0:T(8,128)(2,1)}), bf16[8192,128]{1,0:T(8,128)(2,1)}) %all-gather.10.cloned.1.call-update) | async-done | bytes 2097168 | tf_op jit(solution)/shard_map/all_gather | solution.py:57
  122.8 7.8 convolution_bitcast_fusion.1
  131.4 37.6 %all-gather.12.cloned.1.call-done = bf16[8192,128]{1,0:T(8,128)(2,1)} async-done(((bf16[2048,128]{1,0:T(8,128)(2,1)}), bf16[8192,128]{1,0:T(8,128)(2,1)}) %all-gather.12.cloned.1.call-update) | async-done | bytes 2097168 | tf_op jit(solution)/shard_map/all_gather | solution.py:62
  168.9 7.8 convolution_convert_fusion
  179.3 1.2 multiply_cosine_fusion
  180.5 28.3 %all-gather.14.cloned.1.call-done = bf16[2560,256]{0,1:T(8,128)(2,1)} async-done(((bf16[640,256]{0,1:T(8,128)(2,1)}), bf16[2560,256]{0,1:T(8,128)(2,1)}) %all-gather.14.cloned.1.call-update) | async-done | bytes 1310736 | tf_op jit(solution)/shard_map/all_gather | solution.py:85
  208.8 1.4 fusion.38
  211.6 284.8 %all-gather.16.cloned.1.call-done = bf16[8192,1024]{1,0:T(8,128)(2,1)} async-done(((bf16[2048,1024]{1,0:T(8,128)(2,1)}), bf16[8192,1024]{1,0:T(8,128)(2,1)}) %all-gather.16.cloned.1.call-update) | async-done | bytes 16777232 | tf_op jit(solution)/shard_map/all_gather | solution.py:52
  496.5 16.3 %convolution_bitcast_fusion = f32[80,8,8,128]{3,1,2,0:T(8,128)S(1)} fusion(bf16[8192,1024]{1,0:T(8,128)(2,1)} %all-gather.16.cloned.1.call-done, bf16[640,8192]{1,0:T(8,128)(2,1)} %all-gather.8.cloned.1.call-done, f32[8192]{0:T(1024)S(1)} %convert_element_type.54, f32[640]{0:T(1024)S(1)} %add_rsqrt_fusion), kind=kOutput, calls=%fused_computation.37 | convolution fusion | flops 10758389760 | bytes 29919744 | tf_op jit(solution)/shard_map/dot_general | solution.py:50
  515.2 1.8 pad_maximum_fusion
  517.0 95.3 %while.15 = (s32[]{:T(128)}, f32[8,640]{1,0:T(8,128)S(1)}, f32[8,640]{1,0:T(8,128)S(1)}, f32[8,640,128]{2,1,0:T(8,128)}, s32[640]{0:T(1024)S(1)}, /*index=5*/s32...) while((s32[]{:T(128)}, f32[8,640]{1,0:T(8,128)S(1)}, ...), condition=%wide.region_7.8_spmd.clone, body=%wide.region_3.7_spmd.clone.sunk | while | flops 1723548800 | bytes 100618976 | solution.py:120
  518.6 7.3 fusion.55
  526.0 8.0 fusion.56
  534.5 6.0 fusion.58
  542.2 7.3 fusion.55
  549.5 8.0 fusion.56
  558.0 6.4 fusion.58
  566.1 7.3 fusion.55
  573.4 8.0 fusion.56
  581.9 6.4 fusion.58
  590.0 7.3 fusion.55
  597.3 8.0 fusion.56
  605.8 6.4 fusion.58
  612.2 2.2 copy.24
  614.4 1.3 divide_convert_fusion
  615.7 167.2 %all-gather.20.cloned.1.call-done = bf16[8192,1024]{1,0:T(8,128)(2,1)} async-done(((bf16[2048,1024]{1,0:T(8,128)(2,1)}), bf16[8192,1024]{1,0:T(8,128)(2,1)}) %all-gather.20.cloned.1.call-update) | async-done | bytes 16777232 | tf_op jit(solution)/shard_map/all_gather | solution.py:130
  782.9 63.4 %all-gather.18.cloned.1.call-done = bf16[640,8192]{0,1:T(8,128)(2,1)} async-done(((bf16[640,1024]{0,1:T(8,128)(2,1)}), bf16[640,8192]{0,1:T(8,128)(2,1)}) %all-gather.18.cloned.1.call-update) | async-done | bytes 10485776 | tf_op jit(solution)/shard_map/all_gather | solution.py:132
  846.3 18.8 %add_convert_fusion = bf16[640,1024]{1,0:T(8,128)(2,1)} fusion(bf16[640,1024]{1,0:T(8,128)(2,1)} %param.9, bf16[640,8192]{0,1:T(8,128)(2,1)} %all-gather.18.cloned.1.call-done, bf16[8192,1024]{1,0:T(8,128)(2,1)} %all-gather.20.cloned.1.call-done), kind=kOutput, calls=%fused_computation.33 | convolution fusion | flops 10739384320 | bytes 29884416 | tf_op jit(solution)/shard_map/dot_general | solution.py:131
  (73 shorter events, 14.1 us)
Async XLA Ops:
  6.5 4.7 copy-start.1
  6.5 68.7 %all-gather.8.cloned.1.call-start = ((), (), s32[]{:S(2)}) async-start(), calls=%async_computation | async-start | bytes 11796480 | tf_op jit(solution)/shard_map/all_gather | solution.py:46
  7.3 115.5 %all-gather.10.cloned.1.call-start = ((), (), s32[]{:S(2)}) async-start(), calls=%async_computation.1 | async-start | bytes 2621440 | tf_op jit(solution)/shard_map/all_gather | solution.py:57
  9.2 159.7 %all-gather.12.cloned.1.call-start = ((), (), s32[]{:S(2)}) async-start(), calls=%async_computation.2 | async-start | bytes 2621440 | tf_op jit(solution)/shard_map/all_gather | solution.py:62
  11.2 197.6 %all-gather.14.cloned.1.call-start = ((), (), s32[]{:S(2)}) async-start(), calls=%async_computation.3 | async-start | bytes 1638400 | tf_op jit(solution)/shard_map/all_gather | solution.py:85
  177.6 1.4 copy-start.2
  177.6 318.9 %all-gather.16.cloned.1.call-start = ((), (), s32[]{:S(2)}) async-start(), calls=%async_computation.4 | async-start | bytes 20971520 | tf_op jit(solution)/shard_map/all_gather | solution.py:52
  178.2 604.7 %all-gather.20.cloned.1.call-start = ((), (), s32[]{:S(2)}) async-start(), calls=%async_computation.6 | async-start | bytes 20971520 | tf_op jit(solution)/shard_map/all_gather | solution.py:130
  178.8 667.5 %all-gather.18.cloned.1.call-start = ((), (), s32[]{:S(2)}) async-start(), calls=%async_computation.5 | async-start | bytes 11796480 | tf_op jit(solution)/shard_map/all_gather | solution.py:132
  526.0 8.5 copy-start
  549.5 8.5 copy-start
  573.4 8.5 copy-start
  597.3 8.5 copy-start
Sparse Core Ops, SparseCore 0:
  9.3 65.9 all-gather.7
  76.8 45.9 all-gather.9
  124.4 44.5 all-gather.11
  177.7 31.0 all-gather.13
  210.2 286.1 all-gather.15
  497.9 284.9 all-gather.19
  784.8 61.4 all-gather.17
